TPU v7x, 512 devices: a whole 4x4x16 slice. The times are simulated.
512 devices in a mesh: dp: 64 (over z_lo, x, core), tensor: 8 (over z_hi, y).
Axes of the slice: x: 4, y: 4, z: 16 (z_hi: 2, z_lo: 8; z = z_hi * 8 + z_lo), core: 2. Of those that a mesh axis runs over, the one named last changes fastest.
Arguments:
- visits: bfloat16 [8192, 4096], P('dp'), may hold values from -6 to 6
- notes: bfloat16 [8192, 4096], P('dp'), may hold values from -6 to 6
- visit_weight: bfloat16 [4096, 1024], P('dp', 'tensor'), may hold values from -0.09375 to 0.09375
- note_weight: bfloat16 [4096, 1024], P('dp', 'tensor'), may hold values from -0.09375 to 0.09375
- patient_ids: int32 [8192], replicated, may hold values from 0 to 4095
- loss_grad: float32 [1], replicated, may hold values from 64 to 256
Outputs:
- visit_weight_grad: float32 [4096, 1024], P('dp', 'tensor')
- note_weight_grad: float32 [4096, 1024], P('dp', 'tensor')
Inputs may be any that keep to these rules, and one draw needn't show every extreme that they name: `patient_ids`: pairs with equal ids are positive pairs; every pair is positive with itself.
All inputs are finite; a program needn't handle non-finite values.
Results may differ from a plain program's by a relative error of at most 0.015.
Values may be sent and summed in bfloat16 or wider, within the bound.
A program may use at most 64 MiB of HBM per device.

v0:
```python
import jax
import jax.numpy as jnp
from jax import lax
from jax.sharding import PartitionSpec as P

SCALE = 10.0
BIAS = -2.0
EPS = 1e-06
INNER = (((1,), (1,)), ((), ()))
OUTER = (((0,), (0,)), ((), ()))


def local(visits, notes, visit_weight, note_weight, patient_ids, loss_grad):
    rows = visits.shape[0]
    total = patient_ids.shape[0]
    proj_visit = jnp.dot(
        visits,
        lax.all_gather(visit_weight, "dp", axis=0, tiled=True),
        preferred_element_type=jnp.float32,
    )
    proj_note = jnp.dot(
        notes,
        lax.all_gather(note_weight, "dp", axis=0, tiled=True),
        preferred_element_type=jnp.float32,
    )
    square_parts = (
        lax.all_gather(
            jnp.sum(proj_visit * proj_visit, axis=1)[None, :], "tensor", axis=0, tiled=True
        ),
        lax.all_gather(
            jnp.sum(proj_note * proj_note, axis=1)[None, :], "tensor", axis=0, tiled=True
        ),
    )
    norm_visit = jnp.sqrt(jnp.sum(square_parts[0], axis=0) + EPS)[:, None]
    norm_note = jnp.sqrt(jnp.sum(square_parts[1], axis=0) + EPS)[:, None]
    unit_visit = proj_visit / norm_visit
    unit_note = proj_note / norm_note
    visit_low = unit_visit.astype(jnp.bfloat16)
    note_low = unit_note.astype(jnp.bfloat16)
    offset = lax.axis_index("dp") * rows
    own_ids = lax.dynamic_slice_in_dim(patient_ids, offset, rows, 0)
    factor = SCALE * loss_grad[0] / total

    def weights_of(summed, sign):
        logit = SCALE * summed + BIAS
        return (factor * -sign * jax.nn.sigmoid(-sign * logit)).astype(jnp.bfloat16)

    visit_all, note_all = (
        lax.all_gather(visit_low, "dp", axis=0, tiled=True),
        lax.all_gather(note_low, "dp", axis=0, tiled=True),
    )
    sign = jnp.where(own_ids[:, None] == patient_ids[None, :], 1.0, -1.0).astype(jnp.float32)
    row_part = lax.dot_general(visit_low, note_all, INNER, preferred_element_type=jnp.float32)
    col_part = lax.dot_general(note_low, visit_all, INNER, preferred_element_type=jnp.float32)
    row_sum, col_sum = (
        lax.psum(row_part.astype(jnp.bfloat16), "tensor").astype(jnp.float32),
        lax.psum(col_part.astype(jnp.bfloat16), "tensor").astype(jnp.float32),
    )
    row_weights = weights_of(row_sum, sign)
    col_weights = weights_of(col_sum, sign)
    d_note = jnp.dot(col_weights, visit_all, preferred_element_type=jnp.float32)
    d_visit = jnp.dot(row_weights, note_all, preferred_element_type=jnp.float32)
    dot_parts = (
        lax.all_gather(
            jnp.sum(unit_visit * d_visit, axis=1)[None, :], "tensor", axis=0, tiled=True
        ),
        lax.all_gather(jnp.sum(unit_note * d_note, axis=1)[None, :], "tensor", axis=0, tiled=True),
    )
    dot_visit = jnp.sum(dot_parts[0], axis=0)[:, None]
    dot_note = jnp.sum(dot_parts[1], axis=0)[:, None]
    grad_visit = ((d_visit - unit_visit * dot_visit) / norm_visit).astype(jnp.bfloat16)
    grad_note = ((d_note - unit_note * dot_note) / norm_note).astype(jnp.bfloat16)
    piece = visits
    visit_weight_grad = lax.psum_scatter(
        lax.dot_general(piece, grad_visit, OUTER, preferred_element_type=jnp.float32),
        "dp",
        scatter_dimension=0,
        tiled=True,
    )
    piece = notes
    note_weight_grad = lax.psum_scatter(
        lax.dot_general(piece, grad_note, OUTER, preferred_element_type=jnp.float32),
        "dp",
        scatter_dimension=0,
        tiled=True,
    )
    return (visit_weight_grad, note_weight_grad)


def solution(mesh):
    return jax.shard_map(
        local,
        mesh=mesh,
        in_specs=(P("dp", None), P("dp", None), P("dp", "tensor"), P("dp", "tensor"), P(), P()),
        out_specs=(P("dp", "tensor"), P("dp", "tensor")),
        check_vma=False,
    )
```

profile of v0, /device:TPU:1, one launch (start us, length us, event | category | flops | bytes accessed | tf_op | source)
XLA Modules:
  0.0 1776.0 jit_solution(9918019114257644966)
XLA Ops:
  7.2 0.7 all-gather.13.cloned.1.call-update
  8.0 0.7 all-gather.15.cloned.1.call-update
  8.7 126.4 %all-gather.13.cloned.1.call-done = bf16[4096,128]{1,0:T(8,128)(2,1)} async-done(((bf16[64,128]{1,0:T(8,128)(2,1)}), bf16[4096,128]{1,0:T(8,128)(2,1)}) %all-gather.13.cloned.1.call-update) | async-done | bytes 1048592 | tf_op jit(solution)/shard_map/all_gather | solution.py:18
  135.2 2.1 multiply_reduce_fusion.3
  137.2 37.3 %all-gather.4 = f32[8,1,128]{2,1,0:T(1,128)S(1)} all-gather(f32[1,1,128]{2,1,0:T(1,128)S(1)} %bitcast.23), channel_id=2, replica_groups=mesh['dp'=64,'tensor'=8] {'tensor'}, dimensions={0}, use_global_device_ids=true | all-gather | bytes 4608 | tf_op jit(solution)/shard_map/all_gather | solution.py:27
  175.3 77.0 %all-gather.15.cloned.1.call-done = bf16[4096,128]{1,0:T(8,128)(2,1)} async-done(((bf16[64,128]{1,0:T(8,128)(2,1)}), bf16[4096,128]{1,0:T(8,128)(2,1)}) %all-gather.15.cloned.1.call-update) | async-done | bytes 1048592 | tf_op jit(solution)/shard_map/all_gather | solution.py:23
  252.3 1.8 multiply_reduce_fusion.2
  254.1 37.3 %all-gather.5 = f32[8,1,128]{2,1,0:T(1,128)S(1)} all-gather(f32[1,1,128]{2,1,0:T(1,128)S(1)} %bitcast.24), channel_id=3, replica_groups=mesh['dp'=64,'tensor'=8] {'tensor'}, dimensions={0}, use_global_device_ids=true | all-gather | bytes 4608 | tf_op jit(solution)/shard_map/all_gather | solution.py:30
  291.4 0.6 fusion.16
  292.2 77.2 %all-gather.19.cloned.1.call-done = bf16[8192,128]{0,1:T(8,128)(2,1)} async-done(((bf16[128,128]{0,1:T(8,128)(2,1)}), bf16[8192,128]{0,1:T(8,128)(2,1)}) %all-gather.19.cloned.1.call-update) | async-done | bytes 2097168 | tf_op jit(solution)/shard_map/all_gather | solution.py:49
  369.4 3.6 convolution_convert_fusion
  373.0 113.3 %all-gather.17.cloned.1.call-done = bf16[8192,128]{0,1:T(8,128)(2,1)} async-done(((bf16[128,128]{0,1:T(8,128)(2,1)}), bf16[8192,128]{0,1:T(8,128)(2,1)}) %all-gather.17.cloned.1.call-update) | async-done | bytes 2097168 | tf_op jit(solution)/shard_map/all_gather | solution.py:50
  486.4 3.7 convolution_convert_fusion.1
  491.0 365.3 %all-reduce.3.cloned.1.call-done = (bf16[128,8192]{1,0:T(8,128)(2,1)}, bf16[128,8192]{1,0:T(8,128)(2,1)}) async-done(((bf16[128,8192]{1,0:T(8,128)(2,1)}, bf16[128,8192]{1,0:T(8,128)(2,1)}), (bf16[128,8192]{1,0:T(8,128)(2,1)}, bf16[128,8192]{1,0:T(8,128)(2,1)})) %all-reduce.3.cloned.1.call-update) | async-done | bytes 4194320 | tf_op jit(solution)/shard_map/psum | solution.py:56
  856.3 3.9 multiply_reduce_fusion
  860.2 42.5 %all-gather.7 = f32[8,1,128]{2,1,0:T(1,128)S(1)} all-gather(f32[1,1,128]{2,1,0:T(1,128)S(1)} %bitcast.26), channel_id=5, replica_groups=mesh['dp'=64,'tensor'=8] {'tensor'}, dimensions={0}, use_global_device_ids=true | all-gather | bytes 4608 | tf_op jit(solution)/shard_map/all_gather | solution.py:67
  903.1 1.8 copy.14
  905.0 1.5 copy-done.1
  906.5 3.9 multiply_reduce_fusion.1
  910.4 28.9 %all-gather.6 = f32[8,1,128]{2,1,0:T(1,128)S(1)} all-gather(f32[1,1,128]{2,1,0:T(1,128)S(1)} %bitcast.25), channel_id=4, replica_groups=mesh['dp'=64,'tensor'=8] {'tensor'}, dimensions={0}, use_global_device_ids=true | all-gather | bytes 4608 | tf_op jit(solution)/shard_map/all_gather | solution.py:64
  939.3 1.6 convolution_bitcast_fusion.1
  941.0 1.9 copy.12
  942.9 392.2 %reduce-scatter.9.cloned.1.call-done = f32[64,128]{1,0:T(8,128)} async-done(((f32[4096,128]{1,0:T(8,128)}), f32[64,128]{1,0:T(8,128)}) %reduce-scatter.9.cloned.1.call-update) | async-done | bytes 32784
  1335.1 434.1 %reduce-scatter.7.cloned.1.call-done = f32[64,128]{1,0:T(8,128)} async-done(((f32[4096,128]{1,0:T(8,128)}), f32[64,128]{1,0:T(8,128)}) %reduce-scatter.7.cloned.1.call-update) | async-done | bytes 32784
  (30 shorter events, 1.6 us)
Async XLA Ops:
  7.2 245.1 %copy-start = (bf16[128,4096]{1,0:T(8,128)(2,1)S(1)}, bf16[128,4096]{1,0:T(8,128)(2,1)}, u32[]{:S(2)}) copy-start(bf16[128,4096]{1,0:T(8,128)(2,1)} %param.7) | copy-start | bytes 3145732
  7.2 128.0 %all-gather.13.cloned.1.call-start = ((), (), s32[]{:S(2)}) async-start(), calls=%async_computation.2 | async-start | bytes 1064960 | tf_op jit(solution)/shard_map/all_gather | solution.py:18
  7.9 244.4 %all-gather.15.cloned.1.call-start = ((), (), s32[]{:S(2)}) async-start(), calls=%async_computation.3 | async-start | bytes 1064960 | tf_op jit(solution)/shard_map/all_gather | solution.py:23
  8.7 360.7 %all-gather.19.cloned.1.call-start = ((), (), s32[]{:S(2)}) async-start(), calls=%async_computation.5 | async-start | bytes 2129920 | tf_op jit(solution)/shard_map/all_gather | solution.py:49
  175.3 311.1 %all-gather.17.cloned.1.call-start = ((), (), s32[]{:S(2)}) async-start(), calls=%async_computation.4 | async-start | bytes 2129920 | tf_op jit(solution)/shard_map/all_gather | solution.py:50
  292.1 194.3 %copy-start.3 = (bf16[128,128]{0,1:T(8,128)(2,1)S(1)}, bf16[128,128]{0,1:T(8,128)(2,1)}, u32[]{:S(2)}) copy-start(bf16[128,128]{0,1:T(8,128)(2,1)} %fusion.15) | copy-start | bytes 98308
  292.1 564.2 %all-reduce.3.cloned.1.call-start = ((), (), s32[]{:S(2)}) async-start(), calls=%async_computation.8 | async-start | bytes 8388608 | tf_op jit(solution)/shard_map/psum | solution.py:56
  490.1 0.9 copy-start.4
  490.1 366.2 %copy-start.2 = (bf16[8192,128]{0,1:T(8,128)(2,1)S(1)}, bf16[8192,128]{0,1:T(8,128)(2,1)}, u32[]{:S(2)}) copy-start(bf16[8192,128]{0,1:T(8,128)(2,1)} %all-gather.19.cloned.1.call-done) | copy-start | bytes 6291460
  490.1 845.0 %reduce-scatter.9.cloned.1.call-start = ((), (), s32[]{:S(2)}) async-start(), calls=%async_computation.7 | async-start | bytes 2129920
  904.9 1.6 copy-start.1
  904.9 864.3 %reduce-scatter.7.cloned.1.call-start = ((), (), s32[]{:S(2)}) async-start(), calls=%async_computation.6 | async-start | bytes 2129920
Sparse Core Ops, SparseCore 0:
  10.2 124.9 all-gather.12
  137.3 114.9 all-gather.14
  254.9 114.3 all-gather.18
  371.9 114.4 all-gather.16
  490.2 366.0 all-reduce.2
  905.1 429.9 reduce-scatter.8
  1338.7 430.4 reduce-scatter.6
where the time goes:
time: 1790 us; the launch traced here: 1780 us
  waiting for transfers between devices  1590 us (89%)
  blocking collectives  146 us (8%)
  matrix products  21 us (1%)
    unnamed x9, waiting for transfers between devices  828 us
    psum x1, waiting for transfers between devices, local(): lax.psum(row_part.astype(jnp.bfloat16), 'tensor').astype(jnp.float32)  365 us
    all_gather x1, waiting for transfers between devices, local(): lax.all_gather(visit_weight, 'dp', axis=0, tiled=True)  126 us
    all_gather x1, waiting for transfers between devices, local(): lax.all_gather(note_low, 'dp', axis=0, tiled=True)  113 us
    all_gather x1, waiting for transfers between devices, local(): lax.all_gather(visit_low, 'dp', axis=0, tiled=True)  77.2 us
    all_gather x1, waiting for transfers between devices, local(): lax.all_gather(note_weight, 'dp', axis=0, tiled=True)  77 us
    all_gather x1, blocking collectives, local(): lax.all_gather(jnp.sum(unit_note * d_note, axis=1)[None, :], 'tensor', ax...  42.5 us
    all_gather x1, blocking collectives, local(): lax.all_gather(jnp.sum(proj_note * proj_note, axis=1)[None, :], 'tensor',...  37.3 us
  transfers between devices with their start and end apart: 7, of which 7 were waited for; matrix products, arithmetic and copies ran while one was open for 1% of the time, Pallas kernels for 0%

commit v1 on v0

v1 whole, which is shorter than its diff:
```python
import functools

import jax
import jax.numpy as jnp
from jax import lax
from jax.experimental import pallas as pl
from jax.experimental.pallas import tpu as pltpu
from jax.sharding import PartitionSpec as P

SCALE = 10.0
BIAS = -2.0
EPS = 1e-06
F32 = jnp.float32
LOW = jnp.bfloat16
NT = (((1,), (1,)), ((), ()))
TN = (((0,), (0,)), ((), ()))
NX, NY = 4, 4


def flip(value, bit):
    return 1 - value if bit else value


def kernel(
    total,
    visits, notes, visit_weight, note_weight, own_ids, pair_ids, loss_grad,
    visit_out, note_out,
    heads, projs, proj_own, inverse, units, pairs,
    d_own, d_send, d_recv, d_last_send, d_last_recv, dots,
    own_part, core_send, core_recv, x_send, x_recv, z_own, z_send, z_recv,
    head_sent, head_got, proj_sent, proj_got, pair_sent, pair_got,
    d_sent, d_got, grad_sent, grad_got,
):
    dp, tensor = lax.axis_index("dp"), lax.axis_index("tensor")
    c, x, z = lax.rem(dp, 2), lax.rem(lax.div(dp, 2), NX), lax.div(dp, 2 * NX)
    h, q1, q2 = lax.rem(z, 2), lax.rem(lax.div(z, 2), 2), lax.div(z, 4)
    q = lax.div(z, 2)
    y, half = lax.rem(tensor, NY), lax.div(tensor, NY)

    def pair_of(g):
        return flip(q2, g // 2) * 2 + flip(q1, g % 2)

    def at(zz, xx, cc):
        return ((zz * NX + xx) * 2 + cc, tensor)

    def z_peer(k):
        return at(pair_of(k // 2) * 2 + flip(h, k % 2), x, c)

    def x_right(k):
        return lax.rem(x + k, NX)

    def x_left(k):
        return lax.rem(x + NX - k, NX)

    def x_peer(k):
        return at(z, x_right(k), c)

    def y_right(k):
        return lax.rem(y + k, NY)

    def y_left(k):
        return lax.rem(y + NY - k, NY)

    def y_peer(k):
        return (dp, half * NY + y_right(k))

    core_peer = at(z, x, 1 - c)
    half_peer = (dp, (1 - half) * NY + y)

    started = []

    def send(src, dst, sent, got, peer):
        copy = pltpu.make_async_remote_copy(
            src_ref=src, dst_ref=dst, send_sem=sent, recv_sem=got,
            device_id=peer, device_id_type=pl.DeviceIdType.MESH,
        )
        copy.start()
        started.append(copy)

    def arrived(dst, sent, got, peer):
        pltpu.make_async_remote_copy(
            src_ref=dst, dst_ref=dst, send_sem=sent, recv_sem=got,
            device_id=peer, device_id_type=pl.DeviceIdType.MESH,
        ).wait_recv()

    peers = (
        [z_peer(k) for k in range(1, 8)] + [x_peer(k) for k in range(1, 4)]
        + [y_peer(k) for k in range(1, 4)] + [core_peer, half_peer]
    )
    barrier = pltpu.get_barrier_semaphore()
    for peer in peers:
        pl.semaphore_signal(barrier, inc=1, device_id=peer, device_id_type=pl.DeviceIdType.MESH)

    def gather_start(buf, sent, got):
        mine = buf.at[:, q, h, x, c]
        for k in range(1, 8):
            send(mine, mine, sent.at[k], got.at[k], z_peer(k))

    def gather_rest(buf, sent, got):
        for g in range(4):
            for b in range(2):
                k = 2 * g + b
                if k:
                    arrived(buf.at[:, pair_of(g), flip(h, b), x, c], sent.at[k], got.at[k], z_peer(k))
            block = buf.at[:, pair_of(g), :, x, c]
            for k in (2, 1, 3):
                n = 8 + k * 4 + g
                send(block, block, sent.at[n], got.at[n], x_peer(k))
            send(block, block, sent.at[24 + g], got.at[24 + g], core_peer)
        for g in range(4):
            for k in (1, 3, 2):
                block = buf.at[:, pair_of(g), :, x_left(k), c]
                n = 8 + k * 4 + g
                arrived(block, sent.at[n], got.at[n], x_peer(k))
                m = 24 + k * 4 + g
                send(block, block, sent.at[m], got.at[m], core_peer)
        for g in range(4):
            for k in range(4):
                m = 24 + k * 4 + g
                arrived(
                    buf.at[:, pair_of(g), :, x_left(k), 1 - c], sent.at[m], got.at[m], core_peer
                )

    heads[0, q, h, x, c] = visit_weight[...]
    heads[1, q, h, x, c] = note_weight[...]
    pl.semaphore_wait(barrier, len(peers))
    gather_start(heads, head_sent, head_got)
    gather_rest(heads, head_sent, head_got)

    for a, rows in ((0, visits), (1, notes)):
        head = heads[a].reshape(rows.shape[1], 128)
        proj = jnp.dot(rows[...], head, preferred_element_type=F32)
        proj_own[a] = proj
        projs[a, half, y] = proj.astype(LOW)
    mine = projs.at[:, half, y]
    other = projs.at[:, 1 - half, y]
    send(mine, mine, proj_sent.at[0], proj_got.at[0], half_peer)
    for k in (2, 1, 3):
        send(mine, mine, proj_sent.at[k], proj_got.at[k], y_peer(k))
    arrived(other, proj_sent.at[0], proj_got.at[0], half_peer)
    for k in (2, 1, 3):
        send(other, other, proj_sent.at[4 + k], proj_got.at[4 + k], y_peer(k))
    for k in range(1, 4):
        arrived(projs.at[:, half, y_left(k)], proj_sent.at[k], proj_got.at[k], y_peer(k))
    for k in range(1, 4):
        arrived(projs.at[:, 1 - half, y_left(k)], proj_sent.at[4 + k], proj_got.at[4 + k], y_peer(k))

    def normalised(a, rows):
        parts = [projs[a, t // NY, t % NY, rows, :].astype(F32) for t in range(8)]
        squares = parts[0] * parts[0]
        for part in parts[1:]:
            squares = squares + part * part
        scale = lax.rsqrt(jnp.sum(squares, axis=1, keepdims=True) + EPS)
        return scale, [(part * scale).astype(LOW) for part in parts]

    for a in range(2):
        _, low = normalised(a, pl.ds(pl.multiple_of(tensor * 16, 16), 16))
        for t in range(8):
            pairs[a, q, h, x, c, :, t * 128:(t + 1) * 128] = low[t]
    gather_start(pairs, pair_sent, pair_got)
    for a in range(2):
        scale, low = normalised(a, slice(None))
        inverse[a] = jnp.broadcast_to(scale, (128, 128))
        for t in range(8):
            units[a, :, t * 128:(t + 1) * 128] = low[t]
    gather_rest(pairs, pair_sent, pair_got)

    factor = SCALE * loss_grad[0] / total
    minus_sign = jnp.where(own_ids[...] == pair_ids[...], -1.0, 1.0).astype(F32)
    sums = []
    for a in range(2):
        others = pairs[1 - a].reshape(1024, 1024)
        summed = lax.dot_general(units[a], others, NT, preferred_element_type=F32)
        logit = SCALE * summed + BIAS
        weights = (factor * minus_sign * jax.nn.sigmoid(minus_sign * logit)).astype(LOW)
        sums.append(jnp.sum(weights.astype(F32) * summed, axis=1, keepdims=True))
        d = jnp.dot(weights, others, preferred_element_type=F32)
        for t in range(8):
            piece = d[:, t * 128:(t + 1) * 128]
            d_own[t // NY, t % NY, a] = piece
            d_send[t // NY, t % NY, a] = piece.astype(LOW)
    lane = lax.broadcasted_iota(jnp.int32, (128, 128), 1)
    dots[0] = jnp.transpose(jnp.where(lane == 0, sums[0], sums[1]))[:8]

    for k in (2, 1, 3):
        send(d_send.at[1 - half, y_right(k)], d_recv.at[0, k], d_sent.at[k], d_got.at[k], y_peer(k))
        send(dots.at[0], dots.at[k], d_sent.at[4 + k], d_got.at[4 + k], y_peer(k))
    for k in (2, 1, 3):
        send(d_send.at[half, y_right(k)], d_recv.at[1, k], d_sent.at[8 + k], d_got.at[8 + k], y_peer(k))
    for k in range(1, 4):
        arrived(d_recv.at[0, k], d_sent.at[k], d_got.at[k], y_peer(k))
        arrived(dots.at[k], d_sent.at[4 + k], d_got.at[4 + k], y_peer(k))
    away = d_own[1 - half, y]
    for k in range(1, 4):
        away = away + d_recv[0, k].astype(F32)
    d_last_send[...] = away.astype(LOW)
    send(d_last_send, d_last_recv, d_sent.at[0], d_got.at[0], half_peer)
    dots[4] = dots[0] + dots[1] + dots[2] + dots[3]
    send(dots.at[4], dots.at[5], d_sent.at[4], d_got.at[4], half_peer)
    for k in range(1, 4):
        arrived(d_recv.at[1, k], d_sent.at[8 + k], d_got.at[8 + k], y_peer(k))
    d = d_own[half, y]
    for k in range(1, 4):
        d = d + d_recv[1, k].astype(F32)
    arrived(d_last_recv, d_sent.at[0], d_got.at[0], half_peer)
    arrived(dots.at[5], d_sent.at[4], d_got.at[4], half_peer)
    d = d + d_last_recv[...].astype(F32)
    dot_rows = dots[4] + dots[5]
    grads = []
    for a in range(2):
        dot = jnp.transpose(jnp.broadcast_to(dot_rows[a:a + 1], (128, 128)))
        scale = inverse[a]
        grads.append(((d[a] - proj_own[a] * scale * dot) * scale).astype(LOW))

    for k in (2, 1, 3, 0):
        for a, rows in ((0, visits), (1, notes)):
            for zz in range(8):
                columns = pl.ds(pl.multiple_of((zz * NX + x_right(k)) * 128, 128), 128)
                part = lax.dot_general(rows[:, columns], grads[a], TN, preferred_element_type=F32)
                part = part.reshape(2, 64, 128)
                first, second = part[0], part[1]
                own_part[k, a, zz // 2, zz % 2] = jnp.where(c == 0, first, second)
                core_send[k, a, zz // 2, zz % 2] = jnp.where(c == 0, second, first).astype(LOW)
        send(core_send.at[k], core_recv.at[k], grad_sent.at[k], grad_got.at[k], core_peer)
    for k in (2, 1, 3):
        arrived(core_recv.at[k], grad_sent.at[k], grad_got.at[k], core_peer)
        x_send[k] = (own_part[k] + core_recv[k].astype(F32)).astype(LOW)
        send(x_send.at[k], x_recv.at[k], grad_sent.at[4 + k], grad_got.at[4 + k], x_peer(k))
    arrived(core_recv.at[0], grad_sent.at[0], grad_got.at[0], core_peer)
    z_own[...] = own_part[0] + core_recv[0].astype(F32)
    for k in (1, 3, 2):
        arrived(x_recv.at[k], grad_sent.at[4 + k], grad_got.at[4 + k], x_peer(k))
        z_own[...] += x_recv[k].astype(F32)
    z_send[...] = z_own[...].astype(LOW)
    for k in range(1, 8):
        send(
            z_send.at[:, pair_of(k // 2), flip(h, k % 2)], z_recv.at[k],
            grad_sent.at[8 + k], grad_got.at[8 + k], z_peer(k),
        )
    done = z_own[:, q, h]
    for k in range(1, 8):
        arrived(z_recv.at[k], grad_sent.at[8 + k], grad_got.at[8 + k], z_peer(k))
        done = done + z_recv[k].astype(F32)
    visit_out[...] = done[0]
    note_out[...] = done[1]
    for copy in started:
        copy.wait_send()


def local(visits, notes, visit_weight, note_weight, patient_ids, loss_grad):
    rows = visits.shape[0]
    total = patient_ids.shape[0]
    dp, tensor = lax.axis_index("dp"), lax.axis_index("tensor")
    own_ids = lax.dynamic_slice_in_dim(patient_ids, dp * rows, rows, 0).reshape(rows, 1)
    pair_ids = lax.dynamic_slice_in_dim(
        patient_ids.reshape(total // rows, rows), tensor * 16, 16, 1
    ).reshape(1, -1)
    vmem = pl.BlockSpec(memory_space=pltpu.VMEM)
    grad = jax.ShapeDtypeStruct(visit_weight.shape, F32)
    sems = pltpu.SemaphoreType.DMA
    return pl.pallas_call(
        functools.partial(kernel, total),
        out_shape=(grad, grad),
        in_specs=[vmem] * 6 + [pl.BlockSpec(memory_space=pltpu.SMEM)],
        out_specs=(vmem, vmem),
        scratch_shapes=[
            pltpu.VMEM((2, 4, 2, 4, 2, 64, 128), LOW),
            pltpu.VMEM((2, 2, 4, 128, 128), LOW),
            pltpu.VMEM((2, 128, 128), F32),
            pltpu.VMEM((2, 128, 128), F32),
            pltpu.VMEM((2, 128, 1024), LOW),
            pltpu.VMEM((2, 4, 2, 4, 2, 16, 1024), LOW),
            pltpu.VMEM((2, 4, 2, 128, 128), F32),
            pltpu.VMEM((2, 4, 2, 128, 128), LOW),
            pltpu.VMEM((2, 4, 2, 128, 128), LOW),
            pltpu.VMEM((2, 128, 128), LOW),
            pltpu.VMEM((2, 128, 128), LOW),
            pltpu.VMEM((6, 8, 128), F32),
            pltpu.VMEM((4, 2, 4, 2, 64, 128), F32),
            pltpu.VMEM((4, 2, 4, 2, 64, 128), LOW),
            pltpu.VMEM((4, 2, 4, 2, 64, 128), LOW),
            pltpu.VMEM((4, 2, 4, 2, 64, 128), LOW),
            pltpu.VMEM((4, 2, 4, 2, 64, 128), LOW),
            pltpu.VMEM((2, 4, 2, 64, 128), F32),
            pltpu.VMEM((2, 4, 2, 64, 128), LOW),
            pltpu.VMEM((8, 2, 64, 128), LOW),
            sems((40,)), sems((40,)),
            sems((8,)), sems((8,)),
            sems((40,)), sems((40,)),
            sems((12,)), sems((12,)),
            sems((16,)), sems((16,)),
        ],
        compiler_params=pltpu.CompilerParams(
            collective_id=0, has_side_effects=True, vmem_limit_bytes=48 * 1024 * 1024
        ),
    )(visits, notes, visit_weight, note_weight, own_ids, pair_ids, loss_grad)


def solution(mesh):
    return jax.shard_map(
        local,
        mesh=mesh,
        in_specs=(P("dp", None), P("dp", None), P("dp", "tensor"), P("dp", "tensor"), P(), P()),
        out_specs=(P("dp", "tensor"), P("dp", "tensor")),
        check_vma=False,
    )
```

time: 1790 us -> 138 us (0.08)
  waiting for transfers between devices: 1590 us -> 0 us
  blocking collectives: 146 us -> 0 us
  Pallas kernels: 0 us -> 131 us
  matrix products: 21 us -> 0 us
    unnamed x9 -> x0, waiting for transfers between devices: 828 us -> none
    all_gather x4 -> x0, waiting for transfers between devices: 394 us -> none  [the longest x1 126 us: local(): lax.all_gather(visit_weight, 'dp', axis=0, tiled=True)]
    psum x1 -> x0, waiting for transfers between devices: 365 us -> none  [local(): lax.psum(row_part.astype(jnp.bfloat16), 'tensor').astype(jnp.float32)]
    all_gather x4 -> x0, blocking collectives: 146 us -> none  [the longest x1 42.5 us: local(): lax.all_gather(jnp.sum(unit_note * d_note, axis=1)[None, :], 'tensor', ax...]
    pallas_call x0 -> x1, Pallas kernels: none -> 131 us  [local(): pl.pallas_call(functools.partial(kernel, total), out_shape=(grad, grad),...]
    dot_general x8 -> x0, matrix products: 21 us -> none  [the longest x1 3.86 us: local(): d_note = jnp.dot(col_weights, visit_all, preferred_element_type=jnp.float32)]
  transfers between devices with their start and end apart: 7 -> 0, of which waited for: 7 -> 0; matrix products, arithmetic and copies ran while one was open for 1% -> 0% of each run, Pallas kernels for 0% -> 0%
where the time goes in v1:
time: 138 us; the launch traced here: 137 us
  Pallas kernels  131 us (95%)
  local copies, waits for them, and re-layouts  4.74 us (3%)
    pallas_call x1, Pallas kernels, local(): pl.pallas_call(functools.partial(kernel, total), out_shape=(grad, grad),...  131 us
    unnamed x12, local copies, waits for them, and re-layouts  4.39 us

profile of v1, /device:TPU:1, one launch (start us, length us, event | category | flops | bytes accessed | tf_op | source)
XLA Modules:
  0.0 136.7 jit_solution(2218563822116591770)
XLA Ops:
  0.6 0.0 copy-start
  1.3 0.1 copy-done
  1.4 0.1 dynamic-slice_bitcast_fusion
  1.5 0.1 constant_dynamic-slice_fusion
  1.5 0.1 reshape.15.pair_ids
  1.6 0.0 copy-start.3
  1.6 0.0 copy-start.4
  1.6 0.1 copy.9.own_ids
  1.8 0.6 copy-done.3
  2.4 0.0 copy-done.4
  2.4 0.0 copy-start.1
  2.4 1.2 copy-done.1
  3.6 0.0 copy-start.2
  3.6 1.2 copy-done.2
  4.8 130.6 %shard_map.77 = (f32[64,128]{1,0:T(8,128)S(1)}, f32[64,128]{1,0:T(8,128)S(1)}) custom-call(bf16[128,4096]{1,0:T(8,128)(2,1)S(1)} %copy-done.1, bf16[128,4096]{1,0:T(8,128)(2,1)S(1)} %copy-done.2, bf16[64,128]{1,0:T(8,128)(2,1)S(1)} %copy-done.3, bf16[64,128]{1,0:T(8,128)(2,1)S(1)} %copy-done.4, s32[128,1]{1,0:T(8,128)S(1)} %copy.9.own_ids, ...), custom_call_target="tpu_custom_call" | custom-call | tf_op jit(solution)/shard_map/pallas_call | solution.py:261
  135.5 0.6 copy.13
  136.1 0.6 copy.14
Async XLA Ops:
  0.6 0.8 copy-start
  1.6 0.7 copy-start.3
  1.6 0.7 copy-start.4
  2.4 1.2 copy-start.1
  3.6 1.2 copy-start.2

commit v2 on v1

v2 whole, which is shorter than its diff:
```python
import functools

import jax
import jax.numpy as jnp
from jax import lax
from jax.experimental import pallas as pl
from jax.experimental.pallas import tpu as pltpu
from jax.sharding import PartitionSpec as P

SCALE = 10.0
BIAS = -2.0
EPS = 1e-06
F32 = jnp.float32
LOW = jnp.bfloat16
NT = (((1,), (1,)), ((), ()))
TN = (((0,), (0,)), ((), ()))
NX, NY = 4, 4


def flip(value, bit):
    return 1 - value if bit else value


def kernel(
    total,
    visits_in, notes_in, visit_weight, note_weight, own_ids, pair_ids, loss_grad,
    visit_out, note_out,
    features, heads, projs, proj_own, inverse, units, pairs,
    d_own, d_send, d_recv, d_last, dots,
    own_part, core_send, core_recv, x_send, x_recv, z_own, z_send, z_recv,
    load_done, head_sent, head_got, proj_sent, proj_got, pair_sent, pair_got,
    d_sent, d_got, grad_sent, grad_got,
):
    dp, tensor = lax.axis_index("dp"), lax.axis_index("tensor")
    c, x, z = lax.rem(dp, 2), lax.rem(lax.div(dp, 2), NX), lax.div(dp, 2 * NX)
    z0, z1, z2 = lax.rem(z, 2), lax.rem(lax.div(z, 2), 2), lax.div(z, 4)
    y, half = lax.rem(tensor, NY), lax.div(tensor, NY)
    left, right = lax.rem(x + NX - 1, NX), lax.rem(x + 1, NX)
    beyond = lax.rem(x + 2, NX)

    def low(j):
        return flip(z1, j // 2) * 2 + flip(z0, j % 2)

    def high(f):
        return flip(z2, f)

    def at(zz, xx, cc):
        return ((zz * NX + xx) * 2 + cc, tensor)

    def z_peer(k):
        return at(high(k // 4) * 4 + low(k % 4), x, c)

    def x_right(k):
        return lax.rem(x + k, NX)

    def x_peer(k):
        return at(z, x_right(k), c)

    def y_right(k):
        return lax.rem(y + k, NY)

    def y_left(k):
        return lax.rem(y + NY - k, NY)

    def y_peer(k):
        return (dp, half * NY + y_right(k))

    core_peer = at(z, x, 1 - c)
    half_peer = (dp, (1 - half) * NY + y)
    middle_peer = (((1 - z2) * 4 + low(0)) * NX * 2 + x * 2 + c, (1 - half) * NY + y)

    started = []

    def send(src, dst, sent, got, n, peer):
        copy = pltpu.make_async_remote_copy(
            src_ref=src, dst_ref=dst, send_sem=sent.at[n], recv_sem=got.at[n],
            device_id=peer, device_id_type=pl.DeviceIdType.MESH,
        )
        copy.start()
        started.append(copy)

    def arrived(dst, sent, got, n, peer):
        pltpu.make_async_remote_copy(
            src_ref=dst, dst_ref=dst, send_sem=sent.at[n], recv_sem=got.at[n],
            device_id=peer, device_id_type=pl.DeviceIdType.MESH,
        ).wait_recv()

    peers = (
        [z_peer(k) for k in range(1, 5)] + [x_peer(k) for k in range(1, 4)]
        + [y_peer(k) for k in range(1, 4)] + [core_peer, middle_peer]
    )
    barrier = pltpu.get_barrier_semaphore()
    for peer in peers:
        pl.semaphore_signal(barrier, inc=1, device_id=peer, device_id_type=pl.DeviceIdType.MESH)

    def gather(buf, sent, got):
        def block(j, f, xx):
            return buf.at[high(f), low(j), xx, c]

        def to_x(j, f):
            here = block(j, f, x)
            send(here, here, sent, got, 8 + 2 * j + f, x_peer(1))
            send(here, here, sent, got, 16 + 2 * j + f, x_peer(3))

        def to_core(j, n, xx):
            chunk = buf.at[:, low(j), xx, c]
            send(chunk, chunk, sent, got, 32 + 4 * n + j, core_peer)

        mine = block(0, 0, x)
        send(mine, mine, sent, got, 0, z_peer(4))
        for j in (3, 2, 1):
            send(mine, mine, sent, got, j, z_peer(j))
        to_x(0, 0)
        yield
        for j in (1, 2, 3):
            arrived(block(j, 0, x), sent, got, j, z_peer(j))
            to_x(j, 0)
        yield
        far = block(0, 1, x)
        arrived(far, sent, got, 0, z_peer(4))
        for j in (3, 2, 1):
            send(far, far, sent, got, 4 + j, z_peer(j))
        to_x(0, 1)
        to_core(0, 0, x)
        yield
        for j in range(4):
            theirs = block(j, 0, left)
            arrived(theirs, sent, got, 8 + 2 * j, x_peer(3))
            send(theirs, theirs, sent, got, 24 + 2 * j, x_peer(1))
            arrived(block(j, 0, right), sent, got, 16 + 2 * j, x_peer(1))
        yield
        for j in range(1, 4):
            arrived(block(j, 1, x), sent, got, 4 + j, z_peer(j))
            to_x(j, 1)
            to_core(j, 0, x)
        yield
        for j in range(4):
            theirs = block(j, 1, right)
            arrived(theirs, sent, got, 17 + 2 * j, x_peer(1))
            send(theirs, theirs, sent, got, 25 + 2 * j, x_peer(3))
            arrived(block(j, 1, left), sent, got, 9 + 2 * j, x_peer(3))
            to_core(j, 1, left)
            to_core(j, 2, right)
        yield
        for j in range(4):
            arrived(block(j, 0, beyond), sent, got, 24 + 2 * j, x_peer(3))
            arrived(block(j, 1, beyond), sent, got, 25 + 2 * j, x_peer(1))
            to_core(j, 3, beyond)
        yield
        for n, xx in enumerate((x, left, right, beyond)):
            for j in range(4):
                arrived(buf.at[:, low(j), xx, 1 - c], sent, got, 32 + 4 * n + j, core_peer)
        yield

    def project(a):
        sent, got = proj_sent.at[a], proj_got.at[a]
        head = heads[a].reshape(features.shape[2], 128)
        proj = jnp.dot(features[a], head, preferred_element_type=F32)
        proj_own[a] = proj
        projs[a, half, y] = proj.astype(LOW)
        mine, other = projs.at[a, half, y], projs.at[a, 1 - half, y]
        send(mine, mine, sent, got, 0, half_peer)
        for k in (2, 1, 3):
            send(mine, mine, sent, got, k, y_peer(k))
        yield
        arrived(other, sent, got, 0, half_peer)
        for k in (2, 1, 3):
            send(other, other, sent, got, 4 + k, y_peer(k))
        yield
        for k in range(1, 4):
            arrived(projs.at[a, half, y_left(k)], sent, got, k, y_peer(k))
        for k in range(1, 4):
            arrived(projs.at[a, 1 - half, y_left(k)], sent, got, 4 + k, y_peer(k))
        yield

    def normalised(a, rows):
        parts = [projs[a, t // NY, t % NY, rows, :].astype(F32) for t in range(8)]
        squares = parts[0] * parts[0]
        for part in parts[1:]:
            squares = squares + part * part
        scale = lax.rsqrt(jnp.sum(squares, axis=1, keepdims=True) + EPS)
        return scale, [(part * scale).astype(LOW) for part in parts]

    def first_units(a):
        _, rounded = normalised(a, pl.ds(pl.multiple_of(tensor * 16, 16), 16))
        for t in range(8):
            pairs[a, high(0), low(0), x, c, :, t * 128:(t + 1) * 128] = rounded[t]

    def all_units(a):
        scale, rounded = normalised(a, slice(None))
        inverse[a] = jnp.broadcast_to(scale, (128, 128))
        for t in range(8):
            units[a, :, t * 128:(t + 1) * 128] = rounded[t]

    def embed(a):
        sent, got = d_sent.at[a], d_got.at[a]
        factor = SCALE * loss_grad[0] / total
        minus_sign = jnp.where(own_ids[...] == pair_ids[...], -1.0, 1.0).astype(F32)
        others = pairs[1 - a].reshape(1024, 1024)
        summed = lax.dot_general(units[a], others, NT, preferred_element_type=F32)
        logit = SCALE * summed + BIAS
        weights = (factor * minus_sign * jax.nn.sigmoid(minus_sign * logit)).astype(LOW)
        dot = jnp.sum(weights.astype(F32) * summed, axis=1, keepdims=True)
        d = jnp.dot(weights, others, preferred_element_type=F32)
        for t in range(8):
            piece = d[:, t * 128:(t + 1) * 128]
            d_own[a, t // NY, t % NY] = piece
            d_send[a, t // NY, t % NY] = piece.astype(LOW)
        dots[a, 0] = jnp.transpose(jnp.broadcast_to(dot, (128, 128)))[:8]
        for k in (2, 1, 3):
            send(d_send.at[a, 1 - half, y_right(k)], d_recv.at[a, 0, k], sent, got, k, y_peer(k))
            send(dots.at[a, 0], dots.at[a, k], sent, got, 4 + k, y_peer(k))
        for k in (2, 1, 3):
            send(d_send.at[a, half, y_right(k)], d_recv.at[a, 1, k], sent, got, 8 + k, y_peer(k))
        yield
        away = d_own[a, 1 - half, y]
        for k in range(1, 4):
            arrived(d_recv.at[a, 0, k], sent, got, k, y_peer(k))
            away = away + d_recv[a, 0, k].astype(F32)
        d_last[a, 0] = away.astype(LOW)
        send(d_last.at[a, 0], d_last.at[a, 1], sent, got, 0, half_peer)
        for k in range(1, 4):
            arrived(dots.at[a, k], sent, got, 4 + k, y_peer(k))
        dots[a, 4] = dots[a, 0] + dots[a, 1] + dots[a, 2] + dots[a, 3]
        send(dots.at[a, 4], dots.at[a, 5], sent, got, 4, half_peer)
        yield
        d = d_own[a, half, y]
        for k in range(1, 4):
            arrived(d_recv.at[a, 1, k], sent, got, 8 + k, y_peer(k))
            d = d + d_recv[a, 1, k].astype(F32)
        arrived(d_last.at[a, 1], sent, got, 0, half_peer)
        arrived(dots.at[a, 5], sent, got, 4, half_peer)
        d = d + d_last[a, 1].astype(F32)
        dot = jnp.transpose(jnp.broadcast_to((dots[a, 4] + dots[a, 5])[:1], (128, 128)))
        scale = inverse[a]
        grad = ((d - proj_own[a] * scale * dot) * scale).astype(LOW)

        sent, got = grad_sent.at[a], grad_got.at[a]
        for k in (2, 1, 3, 0):
            for zz in range(8):
                columns = pl.ds(pl.multiple_of((zz * NX + x_right(k)) * 128, 128), 128)
                part = lax.dot_general(features[a, :, columns], grad, TN, preferred_element_type=F32)
                part = part.reshape(2, 64, 128)
                first, second = part[0], part[1]
                own_part[a, k, zz // 4, zz % 4] = jnp.where(c == 0, first, second)
                core_send[a, k, zz // 4, zz % 4] = jnp.where(c == 0, second, first).astype(LOW)
            send(core_send.at[a, k], core_recv.at[a, k], sent, got, k, core_peer)
        yield
        for k in (2, 1, 3):
            arrived(core_recv.at[a, k], sent, got, k, core_peer)
            x_send[a, k] = (own_part[a, k] + core_recv[a, k].astype(F32)).astype(LOW)
            send(x_send.at[a, k], x_recv.at[a, k], sent, got, 4 + k, x_peer(k))
        arrived(core_recv.at[a, 0], sent, got, 0, core_peer)
        z_own[a] = own_part[a, 0] + core_recv[a, 0].astype(F32)
        yield
        for k in (1, 3, 2):
            arrived(x_recv.at[a, k], sent, got, 4 + k, x_peer(k))
        summed = z_own[a]
        for k in (1, 2, 3):
            summed = summed + x_recv[a, k].astype(F32)
        z_own[a] = summed
        z_send[a] = summed.astype(LOW)
        for k in (7, 6, 5, 4, 3, 2, 1):
            there = z_send.at[a, high(k // 4), low(k % 4)]
            send(there, z_recv.at[a, k], sent, got, 8 + k, z_peer(k))
        yield
        done = z_own[a, high(0), low(0)]
        for k in range(1, 8):
            arrived(z_recv.at[a, k], sent, got, 8 + k, z_peer(k))
            done = done + z_recv[a, k].astype(F32)
        (visit_out, note_out)[a][...] = done
        yield

    loads = [
        pltpu.make_async_copy(src, dst, load_done.at[n])
        for n, (src, dst) in enumerate((
            (visit_weight, heads.at[0, high(0), low(0), x, c]),
            (note_weight, heads.at[1, high(0), low(0), x, c]),
            (visits_in, features.at[0]),
            (notes_in, features.at[1]),
        ))
    ]
    for load in loads:
        load.start()
    loads[0].wait()
    loads[1].wait()
    pl.semaphore_wait(barrier, len(peers))

    ga, gb = [gather(heads.at[a], head_sent.at[a], head_got.at[a]) for a in range(2)]
    for _ in range(7):
        next(ga)
        next(gb)
    pa, pb = project(0), project(1)
    loads[2].wait()
    next(ga)
    next(pa)
    loads[3].wait()
    next(gb)
    next(pb)
    next(pa)
    next(pb)
    ga, gb = [gather(pairs.at[a], pair_sent.at[a], pair_got.at[a]) for a in range(2)]
    next(pa)
    first_units(0)
    next(ga)
    next(pb)
    first_units(1)
    next(gb)
    all_units(1)
    next(ga)
    all_units(0)
    ea, eb = embed(0), embed(1)
    order = (
        ga, gb, ga, gb, ga, gb, ga, gb, ga, gb, ga,
        eb, gb, eb, gb, ea, ea, eb, ea, eb, eb, ea, ea, eb, ea,
    )
    for step in order:
        next(step)
    for copy in started:
        copy.wait_send()


def local(visits, notes, visit_weight, note_weight, patient_ids, loss_grad):
    rows = visits.shape[0]
    total = patient_ids.shape[0]
    dp, tensor = lax.axis_index("dp"), lax.axis_index("tensor")
    own_ids = lax.dynamic_slice_in_dim(patient_ids, dp * rows, rows, 0).reshape(rows, 1)
    pair_ids = lax.dynamic_slice_in_dim(
        patient_ids.reshape(total // rows, rows), tensor * 16, 16, 1
    ).reshape(1, -1)
    vmem = pl.BlockSpec(memory_space=pltpu.VMEM)
    hbm = pl.BlockSpec(memory_space=pl.ANY)
    grad = jax.ShapeDtypeStruct(visit_weight.shape, F32)
    sems = pltpu.SemaphoreType.DMA
    return pl.pallas_call(
        functools.partial(kernel, total),
        out_shape=(grad, grad),
        in_specs=[hbm] * 4 + [vmem] * 2 + [pl.BlockSpec(memory_space=pltpu.SMEM)],
        out_specs=(vmem, vmem),
        scratch_shapes=[
            pltpu.VMEM((2,) + visits.shape, LOW),
            pltpu.VMEM((2, 2, 4, 4, 2, 64, 128), LOW),
            pltpu.VMEM((2, 2, 4, 128, 128), LOW),
            pltpu.VMEM((2, 128, 128), F32),
            pltpu.VMEM((2, 128, 128), F32),
            pltpu.VMEM((2, 128, 1024), LOW),
            pltpu.VMEM((2, 2, 4, 4, 2, 16, 1024), LOW),
            pltpu.VMEM((2, 2, 4, 128, 128), F32),
            pltpu.VMEM((2, 2, 4, 128, 128), LOW),
            pltpu.VMEM((2, 2, 4, 128, 128), LOW),
            pltpu.VMEM((2, 2, 128, 128), LOW),
            pltpu.VMEM((2, 6, 8, 128), F32),
            pltpu.VMEM((2, 4, 2, 4, 64, 128), F32),
            pltpu.VMEM((2, 4, 2, 4, 64, 128), LOW),
            pltpu.VMEM((2, 4, 2, 4, 64, 128), LOW),
            pltpu.VMEM((2, 4, 2, 4, 64, 128), LOW),
            pltpu.VMEM((2, 4, 2, 4, 64, 128), LOW),
            pltpu.VMEM((2, 2, 4, 64, 128), F32),
            pltpu.VMEM((2, 2, 4, 64, 128), LOW),
            pltpu.VMEM((2, 8, 64, 128), LOW),
            sems((4,)),
            sems((2, 48)), sems((2, 48)),
            sems((2, 8)), sems((2, 8)),
            sems((2, 48)), sems((2, 48)),
            sems((2, 12)), sems((2, 12)),
            sems((2, 16)), sems((2, 16)),
        ],
        compiler_params=pltpu.CompilerParams(
            collective_id=0, has_side_effects=True, vmem_limit_bytes=48 * 1024 * 1024
        ),
    )(visits, notes, visit_weight, note_weight, own_ids, pair_ids, loss_grad)


def solution(mesh):
    return jax.shard_map(
        local,
        mesh=mesh,
        in_specs=(P("dp", None), P("dp", None), P("dp", "tensor"), P("dp", "tensor"), P(), P()),
        out_specs=(P("dp", "tensor"), P("dp", "tensor")),
        check_vma=False,
    )
```

time: 138 us -> 124 us (0.90)
  the two profiles are of different devices: /device:TPU:1 before, /device:TPU:8 now
where the time goes in v2:
time: 124 us; the launch traced here: 123 us
  Pallas kernels  117 us (94%)
  local copies, waits for them, and re-layouts  4.74 us (4%)
  between operations  1.33 us (1%)
    pallas_call x1, Pallas kernels, local(): pl.pallas_call(functools.partial(kernel, total), out_shape=(grad, grad),...  117 us
    unnamed x12, local copies, waits for them, and re-layouts  4.39 us

profile of v2, /device:TPU:8, one launch (start us, length us, event | category | flops | bytes accessed | tf_op | source)
XLA Modules:
  0.0 123.2 jit_solution(16005226721023145191)
XLA Ops:
  0.6 0.0 copy-start
  1.3 0.1 copy-done
  1.4 0.1 dynamic-slice_bitcast_fusion
  1.5 0.1 constant_dynamic-slice_fusion
  1.5 0.1 reshape.15.pair_ids
  1.6 0.0 copy-start.3
  1.6 0.0 copy-start.4
  1.6 0.1 copy.9.own_ids
  1.8 0.6 copy-done.3
  2.4 0.0 copy-done.4
  2.4 0.0 copy-start.1
  2.4 1.2 copy-done.1
  3.6 0.0 copy-start.2
  3.6 1.2 copy-done.2
  4.8 117.2 %shard_map.77 = (f32[64,128]{1,0:T(8,128)S(1)}, f32[64,128]{1,0:T(8,128)S(1)}) custom-call(bf16[128,4096]{1,0:T(8,128)(2,1)S(1)} %copy-done.1, bf16[128,4096]{1,0:T(8,128)(2,1)S(1)} %copy-done.2, bf16[64,128]{1,0:T(8,128)(2,1)S(1)} %copy-done.3, bf16[64,128]{1,0:T(8,128)(2,1)S(1)} %copy-done.4, s32[128,1]{1,0:T(8,128)S(1)} %copy.9.own_ids, ...), custom_call_target="tpu_custom_call" | custom-call | tf_op jit(solution)/shard_map/pallas_call | solution.py:335
  122.0 0.6 copy.13
  122.6 0.6 copy.14
Async XLA Ops:
  0.6 0.8 copy-start
  1.6 0.7 copy-start.3
  1.6 0.7 copy-start.4
  2.4 1.2 copy-start.1
  3.6 1.2 copy-start.2

commit v3 on v2

--- a/solution.py
+++ b/solution.py
@@ -15,6 +15,9 @@
 NT = (((1,), (1,)), ((), ()))
 TN = (((0,), (0,)), ((), ()))
 NX, NY = 4, 4
+FAR_DIRECT = False
+DOUBLING = False
+ORDER = ('abababababababab', 'abab', 'aababuwababab', 'aBbBb', 'AABBAABBAABA')
 
 
 def flip(value, bit):
@@ -23,9 +26,9 @@
 
 def kernel(
     total,
-    visits_in, notes_in, visit_weight, note_weight, own_ids, pair_ids, loss_grad,
+    visits_in, notes_in, visit_weight, note_weight, ids_in, loss_grad,
     visit_out, note_out,
-    features, heads, projs, proj_own, inverse, units, pairs,
+    ids, moved, signs, features, heads, projs, proj_own, inverse, units, pairs,
     d_own, d_send, d_recv, d_last, dots,
     own_part, core_send, core_recv, x_send, x_recv, z_own, z_send, z_recv,
     load_done, head_sent, head_got, proj_sent, proj_got, pair_sent, pair_got,
@@ -97,10 +100,19 @@
         def block(j, f, xx):
             return buf.at[high(f), low(j), xx, c]
 
+        def to_z(j, f, peer, n):
+            here = block(j, f, x)
+            send(here, here, sent, got, 4 * f + n, z_peer(peer))
+
+        def from_z(j, f, peer):
+            arrived(block(j, f, x), sent, got, 4 * f + j, z_peer(peer))
+
         def to_x(j, f):
             here = block(j, f, x)
             send(here, here, sent, got, 8 + 2 * j + f, x_peer(1))
             send(here, here, sent, got, 16 + 2 * j + f, x_peer(3))
+            if f and FAR_DIRECT:
+                send(here, here, sent, got, 24 + 2 * j + f, x_peer(2))
 
         def to_core(j, n, xx):
             chunk = buf.at[:, low(j), xx, c]
@@ -108,18 +120,19 @@
 
         mine = block(0, 0, x)
         send(mine, mine, sent, got, 0, z_peer(4))
-        for j in (3, 2, 1):
-            send(mine, mine, sent, got, j, z_peer(j))
+        for j in (2, 1) if DOUBLING else (3, 2, 1):
+            to_z(0, 0, j, j)
         to_x(0, 0)
         yield
-        for j in (1, 2, 3):
-            arrived(block(j, 0, x), sent, got, j, z_peer(j))
+        for j in (2, 1, 3) if DOUBLING else (1, 2, 3):
+            from_z(j, 0, 1 if DOUBLING and j == 3 else j)
+            if DOUBLING and j == 2:
+                to_z(2, 0, 1, 3)
             to_x(j, 0)
         yield
-        far = block(0, 1, x)
-        arrived(far, sent, got, 0, z_peer(4))
-        for j in (3, 2, 1):
-            send(far, far, sent, got, 4 + j, z_peer(j))
+        arrived(block(0, 1, x), sent, got, 0, z_peer(4))
+        for j in (2, 1) if DOUBLING else (3, 2, 1):
+            to_z(0, 1, j, j)
         to_x(0, 1)
         to_core(0, 0, x)
         yield
@@ -129,20 +142,23 @@
             send(theirs, theirs, sent, got, 24 + 2 * j, x_peer(1))
             arrived(block(j, 0, right), sent, got, 16 + 2 * j, x_peer(1))
         yield
-        for j in range(1, 4):
-            arrived(block(j, 1, x), sent, got, 4 + j, z_peer(j))
+        for j in (2, 1, 3):
+            from_z(j, 1, 1 if DOUBLING and j == 3 else j)
+            if DOUBLING and j == 2:
+                to_z(2, 1, 1, 3)
             to_x(j, 1)
             to_core(j, 0, x)
         yield
-        for j in range(4):
+        for j in (0, 2, 1, 3):
             theirs = block(j, 1, right)
             arrived(theirs, sent, got, 17 + 2 * j, x_peer(1))
-            send(theirs, theirs, sent, got, 25 + 2 * j, x_peer(3))
+            if not FAR_DIRECT:
+                send(theirs, theirs, sent, got, 25 + 2 * j, x_peer(3))
             arrived(block(j, 1, left), sent, got, 9 + 2 * j, x_peer(3))
             to_core(j, 1, left)
             to_core(j, 2, right)
         yield
-        for j in range(4):
+        for j in (0, 2, 1, 3):
             arrived(block(j, 0, beyond), sent, got, 24 + 2 * j, x_peer(3))
             arrived(block(j, 1, beyond), sent, got, 25 + 2 * j, x_peer(1))
             to_core(j, 3, beyond)
@@ -150,7 +166,6 @@
         for n, xx in enumerate((x, left, right, beyond)):
             for j in range(4):
                 arrived(buf.at[:, low(j), xx, 1 - c], sent, got, 32 + 4 * n + j, core_peer)
-        yield
 
     def project(a):
         sent, got = proj_sent.at[a], proj_got.at[a]
@@ -171,7 +186,6 @@
             arrived(projs.at[a, half, y_left(k)], sent, got, k, y_peer(k))
         for k in range(1, 4):
             arrived(projs.at[a, 1 - half, y_left(k)], sent, got, 4 + k, y_peer(k))
-        yield
 
     def normalised(a, rows):
         parts = [projs[a, t // NY, t % NY, rows, :].astype(F32) for t in range(8)]
@@ -195,7 +209,7 @@
     def embed(a):
         sent, got = d_sent.at[a], d_got.at[a]
         factor = SCALE * loss_grad[0] / total
-        minus_sign = jnp.where(own_ids[...] == pair_ids[...], -1.0, 1.0).astype(F32)
+        minus_sign = signs[...]
         others = pairs[1 - a].reshape(1024, 1024)
         summed = lax.dot_general(units[a], others, NT, preferred_element_type=F32)
         logit = SCALE * summed + BIAS
@@ -246,29 +260,56 @@
                 core_send[a, k, zz // 4, zz % 4] = jnp.where(c == 0, second, first).astype(LOW)
             send(core_send.at[a, k], core_recv.at[a, k], sent, got, k, core_peer)
         yield
-        for k in (2, 1, 3):
-            arrived(core_recv.at[a, k], sent, got, k, core_peer)
-            x_send[a, k] = (own_part[a, k] + core_recv[a, k].astype(F32)).astype(LOW)
-            send(x_send.at[a, k], x_recv.at[a, k], sent, got, 4 + k, x_peer(k))
+        for f in (1, 0):
+            to = high(f)
+            for k in (2, 1, 3):
+                if f:
+                    arrived(core_recv.at[a, k], sent, got, k, core_peer)
+                x_send[a, k, to] = (own_part[a, k, to] + core_recv[a, k, to].astype(F32)).astype(LOW)
+                n = 4 * (2 - f) + k
+                send(x_send.at[a, k, to], x_recv.at[a, k, to], sent, got, n, x_peer(k))
         arrived(core_recv.at[a, 0], sent, got, 0, core_peer)
         z_own[a] = own_part[a, 0] + core_recv[a, 0].astype(F32)
         yield
-        for k in (1, 3, 2):
-            arrived(x_recv.at[a, k], sent, got, 4 + k, x_peer(k))
-        summed = z_own[a]
-        for k in (1, 2, 3):
-            summed = summed + x_recv[a, k].astype(F32)
-        z_own[a] = summed
-        z_send[a] = summed.astype(LOW)
-        for k in (7, 6, 5, 4, 3, 2, 1):
-            there = z_send.at[a, high(k // 4), low(k % 4)]
-            send(there, z_recv.at[a, k], sent, got, 8 + k, z_peer(k))
+        for f in (1, 0):
+            to = high(f)
+            summed = z_own[a, to]
+            for k in (1, 3, 2):
+                arrived(x_recv.at[a, k, to], sent, got, 4 * (2 - f) + k, x_peer(k))
+                summed = summed + x_recv[a, k, to].astype(F32)
+            z_own[a, to] = summed
+            z_send[a, to] = summed.astype(LOW)
+            for k in ((7, 6, 5, 4) if f else (3, 2, 1)):
+                there = z_send.at[a, to, low(k % 4)]
+                send(there, z_recv.at[a, k], sent, got, 12 + k, z_peer(k))
+            if f:
+                yield
         yield
         done = z_own[a, high(0), low(0)]
         for k in range(1, 8):
-            arrived(z_recv.at[a, k], sent, got, 8 + k, z_peer(k))
+            arrived(z_recv.at[a, k], sent, got, 12 + k, z_peer(k))
             done = done + z_recv[a, k].astype(F32)
         (visit_out, note_out)[a][...] = done
+        yield
+
+    def mark_signs():
+        own = jnp.transpose(jnp.broadcast_to(ids[pl.ds(dp, 1), :], (128, 128)))
+        moved[...] = pltpu.roll(ids[...], lax.rem(128 - tensor * 16, 128), 1)
+        lane = lax.div(lax.broadcasted_iota(jnp.int32, (8, 128), 1), 16)
+        packed = jnp.zeros((8, 128), jnp.int32)
+        for k in range(8):
+            part = moved[pl.ds(k, 8, stride=8), :]
+            packed = jnp.where(lane == k, pltpu.roll(part, 16 * k, 1) if k else part, packed)
+        for n in range(8):
+            row = packed[n:n + 1]
+            signs[:, n * 128:(n + 1) * 128] = jnp.where(own == row, -1.0, 1.0).astype(F32)
+
+    def chain(a):
+        yield from gather(heads.at[a], head_sent.at[a], head_got.at[a])
+        loads[2 + a].wait()
+        yield from project(a)
+        first_units(a)
+        yield from gather(pairs.at[a], pair_sent.at[a], pair_got.at[a])
         yield
 
     loads = [
@@ -278,44 +319,23 @@
             (note_weight, heads.at[1, high(0), low(0), x, c]),
             (visits_in, features.at[0]),
             (notes_in, features.at[1]),
+            (ids_in, ids),
         ))
     ]
-    for load in loads:
-        load.start()
+    for n in (4, 0, 1, 2, 3):
+        loads[n].start()
+    loads[4].wait()
+    mark_signs()
     loads[0].wait()
     loads[1].wait()
     pl.semaphore_wait(barrier, len(peers))
 
-    ga, gb = [gather(heads.at[a], head_sent.at[a], head_got.at[a]) for a in range(2)]
-    for _ in range(7):
-        next(ga)
-        next(gb)
-    pa, pb = project(0), project(1)
-    loads[2].wait()
-    next(ga)
-    next(pa)
-    loads[3].wait()
-    next(gb)
-    next(pb)
-    next(pa)
-    next(pb)
-    ga, gb = [gather(pairs.at[a], pair_sent.at[a], pair_got.at[a]) for a in range(2)]
-    next(pa)
-    first_units(0)
-    next(ga)
-    next(pb)
-    first_units(1)
-    next(gb)
-    all_units(1)
-    next(ga)
-    all_units(0)
-    ea, eb = embed(0), embed(1)
-    order = (
-        ga, gb, ga, gb, ga, gb, ga, gb, ga, gb, ga,
-        eb, gb, eb, gb, ea, ea, eb, ea, eb, eb, ea, ea, eb, ea,
-    )
-    for step in order:
-        next(step)
+    steps = {"a": chain(0), "b": chain(1), "A": embed(0), "B": embed(1)}
+    for step in "".join(ORDER):
+        if step in "uw":
+            all_units("uw".index(step))
+        else:
+            next(steps[step])
     for copy in started:
         copy.wait_send()
 
@@ -323,21 +343,19 @@
 def local(visits, notes, visit_weight, note_weight, patient_ids, loss_grad):
     rows = visits.shape[0]
     total = patient_ids.shape[0]
-    dp, tensor = lax.axis_index("dp"), lax.axis_index("tensor")
-    own_ids = lax.dynamic_slice_in_dim(patient_ids, dp * rows, rows, 0).reshape(rows, 1)
-    pair_ids = lax.dynamic_slice_in_dim(
-        patient_ids.reshape(total // rows, rows), tensor * 16, 16, 1
-    ).reshape(1, -1)
     vmem = pl.BlockSpec(memory_space=pltpu.VMEM)
-    hbm = pl.BlockSpec(memory_space=pl.ANY)
+    hbm = pl.BlockSpec(memory_space=pltpu.HBM)
     grad = jax.ShapeDtypeStruct(visit_weight.shape, F32)
     sems = pltpu.SemaphoreType.DMA
     return pl.pallas_call(
         functools.partial(kernel, total),
         out_shape=(grad, grad),
-        in_specs=[hbm] * 4 + [vmem] * 2 + [pl.BlockSpec(memory_space=pltpu.SMEM)],
+        in_specs=[hbm] * 5 + [pl.BlockSpec(memory_space=pltpu.SMEM)],
         out_specs=(vmem, vmem),
         scratch_shapes=[
+            pltpu.VMEM((total // rows, rows), jnp.int32),
+            pltpu.VMEM((total // rows, rows), jnp.int32),
+            pltpu.VMEM((128, 1024), F32),
             pltpu.VMEM((2,) + visits.shape, LOW),
             pltpu.VMEM((2, 2, 4, 4, 2, 64, 128), LOW),
             pltpu.VMEM((2, 2, 4, 128, 128), LOW),
@@ -358,17 +376,17 @@
             pltpu.VMEM((2, 2, 4, 64, 128), F32),
             pltpu.VMEM((2, 2, 4, 64, 128), LOW),
             pltpu.VMEM((2, 8, 64, 128), LOW),
-            sems((4,)),
+            sems((5,)),
             sems((2, 48)), sems((2, 48)),
             sems((2, 8)), sems((2, 8)),
             sems((2, 48)), sems((2, 48)),
             sems((2, 12)), sems((2, 12)),
-            sems((2, 16)), sems((2, 16)),
+            sems((2, 20)), sems((2, 20)),
         ],
         compiler_params=pltpu.CompilerParams(
-            collective_id=0, has_side_effects=True, vmem_limit_bytes=48 * 1024 * 1024
+            collective_id=0, has_side_effects=True, vmem_limit_bytes=60 * 1024 * 1024
         ),
-    )(visits, notes, visit_weight, note_weight, own_ids, pair_ids, loss_grad)
+    )(visits, notes, visit_weight, note_weight, patient_ids.reshape(-1, rows), loss_grad)
 
 
 def solution(mesh):

time: 124 us -> 118 us (0.952)
  the two profiles are of different devices: /device:TPU:8 before, /device:TPU:1 now
where the time goes in v3:
time: 118 us; the launch traced here: 117 us
  Pallas kernels  114 us (97%)
  local copies, waits for them, and re-layouts  2 us (2%)
  between operations  1.29 us (1%)
    pallas_call x1, Pallas kernels, local(): pl.pallas_call(functools.partial(kernel, total), out_shape=(grad, grad),...  114 us

profile of v3, /device:TPU:1, one launch (start us, length us, event | category | flops | bytes accessed | tf_op | source)
XLA Modules:
  0.0 117.3 jit_solution(377349901524781977)
XLA Ops:
  1.3 114.0 %shard_map.77 = (f32[64,128]{1,0:T(8,128)}, f32[64,128]{1,0:T(8,128)}) custom-call(bf16[128,4096]{1,0:T(8,128)(2,1)} %visits_in.1, bf16[128,4096]{1,0:T(8,128)(2,1)} %notes_in.1, bf16[64,128]{1,0:T(8,128)(2,1)} %visit_weight.1, bf16[64,128]{1,0:T(8,128)(2,1)} %note_weight.1, s32[64,128]{1,0:T(8,128)} %bitcast.1, f32[1]{0:T(128)S(6)} %copy.10.loss_grad), custom_call_target="tpu_custom_call" | custom-call | tf_op jit(solution)/shard_map/pallas_call | solution.py:350
  115.3 0.0 copy-start
  115.3 1.4 %copy.11 = f32[64,128]{1,0:T(8,128)} copy(f32[64,128]{1,0:T(8,128)} %get-tuple-element.4) | data formatting | bytes 65536
  116.7 0.0 copy-done
  116.7 0.6 copy.12
Async XLA Ops:
  115.3 1.4 %copy-start = (f32[64,128]{1,0:T(8,128)S(1)}, f32[64,128]{1,0:T(8,128)}, u32[]{:S(2)}) copy-start(f32[64,128]{1,0:T(8,128)} %get-tuple-element.5) | copy-start | bytes 98308

commit v4 on v3

--- a/solution.py
+++ b/solution.py
@@ -15,9 +15,7 @@
 NT = (((1,), (1,)), ((), ()))
 TN = (((0,), (0,)), ((), ()))
 NX, NY = 4, 4
-FAR_DIRECT = False
-DOUBLING = False
-ORDER = ('abababababababab', 'abab', 'aababuwababab', 'aBbBb', 'AABBAABBAABA')
+ORDER = ('aabababababababb', 'cdab', 'aabcdabababdab', 'aBbBbc', 'AABBAABBAABA')
 
 
 def flip(value, bit):
@@ -28,11 +26,11 @@
     total,
     visits_in, notes_in, visit_weight, note_weight, ids_in, loss_grad,
     visit_out, note_out,
-    ids, moved, signs, features, heads, projs, proj_own, inverse, units, pairs,
+    ids, moved, signs, features, heads, projs, firsts, proj_own, inverse, units, pairs,
     d_own, d_send, d_recv, d_last, dots,
     own_part, core_send, core_recv, x_send, x_recv, z_own, z_send, z_recv,
     load_done, head_sent, head_got, proj_sent, proj_got, pair_sent, pair_got,
-    d_sent, d_got, grad_sent, grad_got,
+    d_sent, d_got, grad_sent, grad_got, known,
 ):
     dp, tensor = lax.axis_index("dp"), lax.axis_index("tensor")
     c, x, z = lax.rem(dp, 2), lax.rem(lax.div(dp, 2), NX), lax.div(dp, 2 * NX)
@@ -111,8 +109,6 @@
             here = block(j, f, x)
             send(here, here, sent, got, 8 + 2 * j + f, x_peer(1))
             send(here, here, sent, got, 16 + 2 * j + f, x_peer(3))
-            if f and FAR_DIRECT:
-                send(here, here, sent, got, 24 + 2 * j + f, x_peer(2))
 
         def to_core(j, n, xx):
             chunk = buf.at[:, low(j), xx, c]
@@ -120,18 +116,16 @@
 
         mine = block(0, 0, x)
         send(mine, mine, sent, got, 0, z_peer(4))
-        for j in (2, 1) if DOUBLING else (3, 2, 1):
+        for j in (3, 2, 1):
             to_z(0, 0, j, j)
         to_x(0, 0)
         yield
-        for j in (2, 1, 3) if DOUBLING else (1, 2, 3):
-            from_z(j, 0, 1 if DOUBLING and j == 3 else j)
-            if DOUBLING and j == 2:
-                to_z(2, 0, 1, 3)
+        for j in (1, 2, 3):
+            from_z(j, 0, j)
             to_x(j, 0)
         yield
         arrived(block(0, 1, x), sent, got, 0, z_peer(4))
-        for j in (2, 1) if DOUBLING else (3, 2, 1):
+        for j in (3, 2, 1):
             to_z(0, 1, j, j)
         to_x(0, 1)
         to_core(0, 0, x)
@@ -143,17 +137,14 @@
             arrived(block(j, 0, right), sent, got, 16 + 2 * j, x_peer(1))
         yield
         for j in (2, 1, 3):
-            from_z(j, 1, 1 if DOUBLING and j == 3 else j)
-            if DOUBLING and j == 2:
-                to_z(2, 1, 1, 3)
+            from_z(j, 1, j)
             to_x(j, 1)
             to_core(j, 0, x)
         yield
         for j in (0, 2, 1, 3):
             theirs = block(j, 1, right)
             arrived(theirs, sent, got, 17 + 2 * j, x_peer(1))
-            if not FAR_DIRECT:
-                send(theirs, theirs, sent, got, 25 + 2 * j, x_peer(3))
+            send(theirs, theirs, sent, got, 25 + 2 * j, x_peer(3))
             arrived(block(j, 1, left), sent, got, 9 + 2 * j, x_peer(3))
             to_core(j, 1, left)
             to_core(j, 2, right)
@@ -173,6 +164,28 @@
         proj = jnp.dot(features[a], head, preferred_element_type=F32)
         proj_own[a] = proj
         projs[a, half, y] = proj.astype(LOW)
+        if a == 0:
+            pl.semaphore_wait(known, 3)
+        for f in (1, 0):
+            for k in (2, 1, 3, 0):
+                peer = flip(half, f) * NY + y_right(k)
+                part = projs.at[a, half, y, pl.ds(pl.multiple_of(peer * 16, 16), 16)]
+                if f or k:
+                    send(part, firsts.at[a, half, y], sent, got, 8 + 4 * f + k, (dp, peer))
+        firsts[a, half, y] = projs[a, half, y, pl.ds(pl.multiple_of(tensor * 16, 16), 16), :]
+        yield
+        for f in (0, 1):
+            for k in range(4):
+                if f or k:
+                    peer = flip(half, f) * NY + y_right(k)
+                    slot = firsts.at[a, flip(half, f), y_left(k)]
+                    arrived(slot, sent, got, 8 + 4 * f + k, (dp, peer))
+        _, rounded = normalised([firsts[a, t // NY, t % NY] for t in range(8)])
+        for t in range(8):
+            pairs[a, high(0), low(0), x, c, :, t * 128:(t + 1) * 128] = rounded[t]
+
+    def spread(a):
+        sent, got = proj_sent.at[a], proj_got.at[a]
         mine, other = projs.at[a, half, y], projs.at[a, 1 - half, y]
         send(mine, mine, sent, got, 0, half_peer)
         for k in (2, 1, 3):
@@ -186,25 +199,19 @@
             arrived(projs.at[a, half, y_left(k)], sent, got, k, y_peer(k))
         for k in range(1, 4):
             arrived(projs.at[a, 1 - half, y_left(k)], sent, got, 4 + k, y_peer(k))
-
-    def normalised(a, rows):
-        parts = [projs[a, t // NY, t % NY, rows, :].astype(F32) for t in range(8)]
+        scale, rounded = normalised([projs[a, t // NY, t % NY] for t in range(8)])
+        inverse[a] = jnp.broadcast_to(scale, (128, 128))
+        for t in range(8):
+            units[a, :, t * 128:(t + 1) * 128] = rounded[t]
+        yield
+
+    def normalised(parts):
+        parts = [part.astype(F32) for part in parts]
         squares = parts[0] * parts[0]
         for part in parts[1:]:
             squares = squares + part * part
         scale = lax.rsqrt(jnp.sum(squares, axis=1, keepdims=True) + EPS)
         return scale, [(part * scale).astype(LOW) for part in parts]
-
-    def first_units(a):
-        _, rounded = normalised(a, pl.ds(pl.multiple_of(tensor * 16, 16), 16))
-        for t in range(8):
-            pairs[a, high(0), low(0), x, c, :, t * 128:(t + 1) * 128] = rounded[t]
-
-    def all_units(a):
-        scale, rounded = normalised(a, slice(None))
-        inverse[a] = jnp.broadcast_to(scale, (128, 128))
-        for t in range(8):
-            units[a, :, t * 128:(t + 1) * 128] = rounded[t]
 
     def embed(a):
         sent, got = d_sent.at[a], d_got.at[a]
@@ -305,10 +312,15 @@
             signs[:, n * 128:(n + 1) * 128] = jnp.where(own == row, -1.0, 1.0).astype(F32)
 
     def chain(a):
-        yield from gather(heads.at[a], head_sent.at[a], head_got.at[a])
+        for n, _ in enumerate(gather(heads.at[a], head_sent.at[a], head_got.at[a])):
+            if a == 0 and n == 2:
+                for k in range(1, 4):
+                    pl.semaphore_signal(
+                        known, inc=1, device_id=y_peer(k), device_id_type=pl.DeviceIdType.MESH
+                    )
+            yield
         loads[2 + a].wait()
         yield from project(a)
-        first_units(a)
         yield from gather(pairs.at[a], pair_sent.at[a], pair_got.at[a])
         yield
 
@@ -330,12 +342,11 @@
     loads[1].wait()
     pl.semaphore_wait(barrier, len(peers))
 
-    steps = {"a": chain(0), "b": chain(1), "A": embed(0), "B": embed(1)}
+    steps = {
+        "a": chain(0), "b": chain(1), "c": spread(0), "d": spread(1), "A": embed(0), "B": embed(1),
+    }
     for step in "".join(ORDER):
-        if step in "uw":
-            all_units("uw".index(step))
-        else:
-            next(steps[step])
+        next(steps[step])
     for copy in started:
         copy.wait_send()
 
@@ -359,6 +370,7 @@
             pltpu.VMEM((2,) + visits.shape, LOW),
             pltpu.VMEM((2, 2, 4, 4, 2, 64, 128), LOW),
             pltpu.VMEM((2, 2, 4, 128, 128), LOW),
+            pltpu.VMEM((2, 2, 4, 16, 128), LOW),
             pltpu.VMEM((2, 128, 128), F32),
             pltpu.VMEM((2, 128, 128), F32),
             pltpu.VMEM((2, 128, 1024), LOW),
@@ -378,10 +390,11 @@
             pltpu.VMEM((2, 8, 64, 128), LOW),
             sems((5,)),
             sems((2, 48)), sems((2, 48)),
-            sems((2, 8)), sems((2, 8)),
+            sems((2, 16)), sems((2, 16)),
             sems((2, 48)), sems((2, 48)),
             sems((2, 12)), sems((2, 12)),
             sems((2, 20)), sems((2, 20)),
+            pltpu.SemaphoreType.REGULAR,
         ],
         compiler_params=pltpu.CompilerParams(
             collective_id=0, has_side_effects=True, vmem_limit_bytes=60 * 1024 * 1024

time: 118 us -> 113 us (0.958)
  Pallas kernels: 114 us -> 110 us
    pallas_call x1, Pallas kernels: 114 us -> 110 us  [local(): pl.pallas_call(functools.partial(kernel, total), out_shape=(grad, grad),...]
where the time goes in v4:
time: 113 us
  Pallas kernels  110 us (97%)
  local copies, waits for them, and re-layouts  2 us (2%)
  between operations  1.29 us (1%)
    pallas_call x1, Pallas kernels, local(): pl.pallas_call(functools.partial(kernel, total), out_shape=(grad, grad),...  110 us

profile of v4, /device:TPU:1, one launch (start us, length us, event | category | flops | bytes accessed | tf_op | source)
XLA Modules:
  0.0 113.2 jit_solution(11141684221959826654)
XLA Ops:
  1.3 110.0 %shard_map.77 = (f32[64,128]{1,0:T(8,128)}, f32[64,128]{1,0:T(8,128)}) custom-call(bf16[128,4096]{1,0:T(8,128)(2,1)} %visits_in.1, bf16[128,4096]{1,0:T(8,128)(2,1)} %notes_in.1, bf16[64,128]{1,0:T(8,128)(2,1)} %visit_weight.1, bf16[64,128]{1,0:T(8,128)(2,1)} %note_weight.1, s32[64,128]{1,0:T(8,128)} %bitcast.1, f32[1]{0:T(128)S(6)} %copy.10.loss_grad), custom_call_target="tpu_custom_call" | custom-call | tf_op jit(solution)/shard_map/pallas_call | solution.py:361
  111.2 0.0 copy-start
  111.3 1.4 %copy.11 = f32[64,128]{1,0:T(8,128)} copy(f32[64,128]{1,0:T(8,128)} %get-tuple-element.4) | data formatting | bytes 65536
  112.6 0.0 copy-done
  112.6 0.6 copy.12
Async XLA Ops:
  111.2 1.4 %copy-start = (f32[64,128]{1,0:T(8,128)S(1)}, f32[64,128]{1,0:T(8,128)}, u32[]{:S(2)}) copy-start(f32[64,128]{1,0:T(8,128)} %get-tuple-element.5) | copy-start | bytes 98308

commit v5 on v4

--- a/solution.py
+++ b/solution.py
@@ -15,7 +15,13 @@
 NT = (((1,), (1,)), ((), ()))
 TN = (((0,), (0,)), ((), ()))
 NX, NY = 4, 4
-ORDER = ('aabababababababb', 'cdab', 'aabcdabababdab', 'aBbBbc', 'AABBAABBAABA')
+ORDER = (
+    "aabababababababb",
+    "cdab",
+    "aabcdabababdab",
+    "aBbBbc",
+    "AABBAABBABAABA",
+)
 
 
 def flip(value, bit):
@@ -28,7 +34,7 @@
     visit_out, note_out,
     ids, moved, signs, features, heads, projs, firsts, proj_own, inverse, units, pairs,
     d_own, d_send, d_recv, d_last, dots,
-    own_part, core_send, core_recv, x_send, x_recv, z_own, z_send, z_recv,
+    own_part, core_send, core_recv, x_send, x_recv, z_own, z_send, z_recv, z_last,
     load_done, head_sent, head_got, proj_sent, proj_got, pair_sent, pair_got,
     d_sent, d_got, grad_sent, grad_got, known,
 ):
@@ -286,17 +292,21 @@
                 summed = summed + x_recv[a, k, to].astype(F32)
             z_own[a, to] = summed
             z_send[a, to] = summed.astype(LOW)
-            for k in ((7, 6, 5, 4) if f else (3, 2, 1)):
-                there = z_send.at[a, to, low(k % 4)]
-                send(there, z_recv.at[a, k], sent, got, 12 + k, z_peer(k))
+            for j in (3, 2, 1):
+                there = z_send.at[a, to, low(j)]
+                send(there, z_recv.at[a, j, to], sent, got, 4 * (4 - f) + j, z_peer(j))
+            yield
+        for f in (1, 0):
+            done = z_own[a, high(f), low(0)]
+            for j in (1, 2, 3):
+                arrived(z_recv.at[a, j, high(f)], sent, got, 4 * (4 - f) + j, z_peer(j))
+                done = done + z_recv[a, j, high(f)].astype(F32)
             if f:
+                z_last[a, 0] = done.astype(LOW)
+                send(z_last.at[a, 0], z_last.at[a, 1], sent, got, 12, z_peer(4))
                 yield
-        yield
-        done = z_own[a, high(0), low(0)]
-        for k in range(1, 8):
-            arrived(z_recv.at[a, k], sent, got, 12 + k, z_peer(k))
-            done = done + z_recv[a, k].astype(F32)
-        (visit_out, note_out)[a][...] = done
+        arrived(z_last.at[a, 1], sent, got, 12, z_peer(4))
+        (visit_out, note_out)[a][...] = done + z_last[a, 1].astype(F32)
         yield
 
     def mark_signs():
@@ -387,7 +397,8 @@
             pltpu.VMEM((2, 4, 2, 4, 64, 128), LOW),
             pltpu.VMEM((2, 2, 4, 64, 128), F32),
             pltpu.VMEM((2, 2, 4, 64, 128), LOW),
-            pltpu.VMEM((2, 8, 64, 128), LOW),
+            pltpu.VMEM((2, 4, 2, 64, 128), LOW),
+            pltpu.VMEM((2, 2, 64, 128), LOW),
             sems((5,)),
             sems((2, 48)), sems((2, 48)),
             sems((2, 16)), sems((2, 16)),

time: 113 us -> 112 us (level)
    pallas_call x1, Pallas kernels: 110 us -> 109 us  [local(): pl.pallas_call(functools.partial(kernel, total), out_shape=(grad, grad),...]
where the time goes in v5:
time: 112 us
  Pallas kernels  109 us (97%)
  local copies, waits for them, and re-layouts  2 us (2%)
  between operations  1.29 us (1%)
    pallas_call x1, Pallas kernels, local(): pl.pallas_call(functools.partial(kernel, total), out_shape=(grad, grad),...  109 us

profile of v5, /device:TPU:1, one launch (start us, length us, event | category | flops | bytes accessed | tf_op | source)
XLA Modules:
  0.0 112.0 jit_solution(4688904957228191720)
XLA Ops:
  1.3 108.7 %shard_map.77 = (f32[64,128]{1,0:T(8,128)}, f32[64,128]{1,0:T(8,128)}) custom-call(bf16[128,4096]{1,0:T(8,128)(2,1)} %visits_in.1, bf16[128,4096]{1,0:T(8,128)(2,1)} %notes_in.1, bf16[64,128]{1,0:T(8,128)(2,1)} %visit_weight.1, bf16[64,128]{1,0:T(8,128)(2,1)} %note_weight.1, s32[64,128]{1,0:T(8,128)} %bitcast.1, f32[1]{0:T(128)S(6)} %copy.10.loss_grad), custom_call_target="tpu_custom_call" | custom-call | tf_op jit(solution)/shard_map/pallas_call | solution.py:371
  110.0 0.0 copy-start
  110.0 1.4 %copy.11 = f32[64,128]{1,0:T(8,128)} copy(f32[64,128]{1,0:T(8,128)} %get-tuple-element.4) | data formatting | bytes 65536
  111.4 0.0 copy-done
  111.4 0.6 copy.12
Async XLA Ops:
  110.0 1.4 %copy-start = (f32[64,128]{1,0:T(8,128)S(1)}, f32[64,128]{1,0:T(8,128)}, u32[]{:S(2)}) copy-start(f32[64,128]{1,0:T(8,128)} %get-tuple-element.5) | copy-start | bytes 98308

commit v6 on v5

--- a/solution.py
+++ b/solution.py
@@ -19,7 +19,7 @@
     "aabababababababb",
     "cdab",
     "aabcdabababdab",
-    "aBbBbc",
+    "aBbcBb",
     "AABBAABBABAABA",
 )
 

time: 112 us -> 112 us (level)
  no operation moved by 1% of the time
where the time goes in v6:
time: 112 us
  Pallas kernels  109 us (97%)
  local copies, waits for them, and re-layouts  2 us (2%)
  between operations  1.29 us (1%)
    pallas_call x1, Pallas kernels, local(): pl.pallas_call(functools.partial(kernel, total), out_shape=(grad, grad),...  109 us

profile of v6, /device:TPU:1, one launch (start us, length us, event | category | flops | bytes accessed | tf_op | source)
XLA Modules:
  0.0 112.0 jit_solution(18299595175225889340)
XLA Ops:
  1.3 108.8 %shard_map.77 = (f32[64,128]{1,0:T(8,128)}, f32[64,128]{1,0:T(8,128)}) custom-call(bf16[128,4096]{1,0:T(8,128)(2,1)} %visits_in.1, bf16[128,4096]{1,0:T(8,128)(2,1)} %notes_in.1, bf16[64,128]{1,0:T(8,128)(2,1)} %visit_weight.1, bf16[64,128]{1,0:T(8,128)(2,1)} %note_weight.1, s32[64,128]{1,0:T(8,128)} %bitcast.1, f32[1]{0:T(128)S(6)} %copy.10.loss_grad), custom_call_target="tpu_custom_call" | custom-call | tf_op jit(solution)/shard_map/pallas_call | solution.py:371
  110.0 0.0 copy-start
  110.0 1.4 %copy.11 = f32[64,128]{1,0:T(8,128)} copy(f32[64,128]{1,0:T(8,128)} %get-tuple-element.4) | data formatting | bytes 65536
  111.4 0.0 copy-done
  111.4 0.6 copy.12
Async XLA Ops:
  110.0 1.4 %copy-start = (f32[64,128]{1,0:T(8,128)S(1)}, f32[64,128]{1,0:T(8,128)}, u32[]{:S(2)}) copy-start(f32[64,128]{1,0:T(8,128)} %get-tuple-element.5) | copy-start | bytes 98308
